TPU v7x, 32 devices: a whole 2x2x4 slice. The times are simulated.
32 devices in a mesh: groups: 2 (over y), gx: 4 (over z), gy: 4 (over x, core).
Axes of the slice: x: 2, y: 2, z: 4, core: 2. Of those that a mesh axis runs over, the one named last changes fastest.
Arguments:
- populations: float32 [19, 64, 64, 128], P(None, ('groups', 'gx'), 'gy'), parts along dimension 1, may hold values from 0 to 1.1, as said below
- fluid_mask: int32 [64, 64, 128], P(('groups', 'gx'), 'gy'), parts along dimension 0, may hold values 0 or 1
- wet_class: int32 [64, 64, 128], P(('groups', 'gx'), 'gy'), parts along dimension 0, may hold values from 0 to 3
- wall_potential: float32 [8], P('groups'), parts along dimension 0, may hold values from 0 to 1
- relax_rates: float32 [19], replicated, may hold values from 0.8 to 1.6
Outputs:
- populations_out: float32 [19, 64, 64, 128], P(None, ('groups', 'gx'), 'gy'), parts along dimension 1
- velocity: float32 [3, 64, 64, 128], P(None, ('groups', 'gx'), 'gy'), parts along dimension 1
There are 2 independent parts, one for each index of `groups`. A program takes and returns all parts, laid end to end along the dimension named above; an argument that names none is the same for every part. Nothing has to cross between parts.
Inputs may be any that keep to these rules, and one draw needn't show every extreme that they name: `populations`: every population is positive.
All inputs are finite; a program needn't handle non-finite values. No bound on the sum of `fluid_mask` on one device may be relied on, other than what follows from the above.
Results may differ from a plain program's by a relative error of at most 0.0003.
Values sent between devices are 32-bit elements; how exact they have to be, the bound alone decides.
A program may use at most 64 MiB of HBM per device.

v0:
```python
import functools

import jax
import jax.numpy as jnp
from jax import lax
from jax.experimental import pallas as pl
from jax.experimental.pallas import tpu as pltpu
from jax.sharding import PartitionSpec as P

WET_CLASSES = 4
STEPS = 4
COUPLING = 2.5
PAD = 8
VEL = [
    (0, 0, 0),
    (1, 0, 0),
    (-1, 0, 0),
    (0, 1, 0),
    (0, -1, 0),
    (0, 0, 1),
    (0, 0, -1),
    (1, 1, 0),
    (-1, -1, 0),
    (1, -1, 0),
    (-1, 1, 0),
    (1, 0, 1),
    (-1, 0, -1),
    (1, 0, -1),
    (-1, 0, 1),
    (0, 1, 1),
    (0, -1, -1),
    (0, 1, -1),
    (0, -1, 1),
]
INDEX = {v: k for k, v in enumerate(VEL)}
OPP = [INDEX[(-a, -b, -c)] for a, b, c in VEL]
ORDER = (
    [k for k in range(19) if VEL[k][0] == 1]
    + [k for k in range(19) if VEL[k][0] == -1]
    + [k for k in range(19) if VEL[k][0] == 0]
)
PLACE = [ORDER.index(k) for k in range(19)]
CROSS = [[k for k in range(19) if VEL[k][1] == s] for s in (-1, 1)]
CORNERS = [(1, 1), (1, -1), (-1, 1), (-1, -1)]
SENDS = [(1, 0), (-1, 0), (0, 1), (0, -1)] + CORNERS


def roll_z(value, step):
    if step == 0:
        return value
    return pltpu.roll(value, step % value.shape[-1], axis=value.ndim - 1)


def to_moments(f):
    g = lambda *v: f[INDEX[v]]
    m = {}

    def plane(pp, mm, pm, mp):
        a, b, c, d = pp + mm, pm + mp, pp - mm, pm - mp
        return a + b, a - b, c + d, c - d

    m["xxyy"], m["xy"], m["xyy"], m["yxx"] = plane(
        g(1, 1, 0), g(-1, -1, 0), g(1, -1, 0), g(-1, 1, 0)
    )
    m["xxzz"], m["xz"], m["xzz"], m["zxx"] = plane(
        g(1, 0, 1), g(-1, 0, -1), g(1, 0, -1), g(-1, 0, 1)
    )
    m["yyzz"], m["yz"], m["yzz"], m["zyy"] = plane(
        g(0, 1, 1), g(0, -1, -1), g(0, 1, -1), g(0, -1, 1)
    )
    sx, dx = f[1] + f[2], f[1] - f[2]
    sy, dy = f[3] + f[4], f[3] - f[4]
    sz, dz = f[5] + f[6], f[5] - f[6]
    m["xx"] = sx + (m["xxyy"] + m["xxzz"])
    m["yy"] = sy + (m["xxyy"] + m["yyzz"])
    m["zz"] = sz + (m["xxzz"] + m["yyzz"])
    m["x"] = dx + (m["xyy"] + m["xzz"])
    m["y"] = dy + (m["yxx"] + m["yzz"])
    m["z"] = dz + (m["zxx"] + m["zyy"])
    m["1"] = ((f[0] + sx) + (sy + sz)) + ((m["xxyy"] + m["xxzz"]) + m["yyzz"])
    return m


def from_moments(m):
    f = [None] * 19

    def plane(even, cross, first, second, v):
        a, b = 0.25 * (even + cross), 0.25 * (even - cross)
        c, d = 0.25 * (first + second), 0.25 * (first - second)
        values = (a + c, a - c, b + d, b - d)
        for velocity, value in zip(v, values):
            f[INDEX[velocity]] = value

    plane(m["xxyy"], m["xy"], m["xyy"], m["yxx"], [(1, 1, 0), (-1, -1, 0), (1, -1, 0), (-1, 1, 0)])
    plane(m["xxzz"], m["xz"], m["xzz"], m["zxx"], [(1, 0, 1), (-1, 0, -1), (1, 0, -1), (-1, 0, 1)])
    plane(m["yyzz"], m["yz"], m["yzz"], m["zyy"], [(0, 1, 1), (0, -1, -1), (0, 1, -1), (0, -1, 1)])
    sx = m["xx"] - (m["xxyy"] + m["xxzz"])
    sy = m["yy"] - (m["xxyy"] + m["yyzz"])
    sz = m["zz"] - (m["xxzz"] + m["yyzz"])
    dx = m["x"] - (m["xyy"] + m["xzz"])
    dy = m["y"] - (m["yxx"] + m["yzz"])
    dz = m["z"] - (m["zxx"] + m["zyy"])
    f[1], f[2] = 0.5 * (sx + dx), 0.5 * (sx - dx)
    f[3], f[4] = 0.5 * (sy + dy), 0.5 * (sy - dy)
    f[5], f[6] = 0.5 * (sz + dz), 0.5 * (sz - dz)
    f[0] = (m["1"] - (sx + sy)) - (sz + ((m["xxyy"] + m["xxzz"]) + m["yyzz"]))
    return f


NAMES = [
    "1", "x", "y", "z", "xy", "xz", "yz", "xx", "yy", "zz",
    "xyy", "xzz", "yxx", "yzz", "zxx", "zyy", "xxyy", "xxzz", "yyzz",
]


EQUIL_SCALE = [1.0] * 10 + [1.0 / 3.0] * 6 + [1.0] * 3
SOURCE_SCALE = [1.0] * 7 + [2.0] * 3 + [1.0 / 3.0] * 6 + [1.0] * 3


def collide(f, fluid, near, coef):
    third = 1.0 / 3.0
    m = to_moments(f)
    here = near(0, 0)
    xp, xm, yp, ym = near(1, 0), near(-1, 0), near(0, 1), near(0, -1)
    dx, dy = xp - xm, yp - ym
    ring = (2.0 * here + (xp + xm)) + (yp + ym)
    pp, pm, mp, mm = near(1, 1), near(1, -1), near(-1, 1), near(-1, -1)
    a, b = pp - mm, pm - mp
    scale = (COUPLING / 36.0) * here
    fx = scale * ((2.0 * dx + (a + b)) + (roll_z(dx, 1) + roll_z(dx, -1)))
    fy = scale * ((2.0 * dy + (a - b)) + (roll_z(dy, 1) + roll_z(dy, -1)))
    fz = scale * (roll_z(ring, -1) - roll_z(ring, 1))
    rho = jnp.where(fluid, m["1"], 1.0)
    inv = 1.0 / rho
    jx, jy, jz = m["x"] + 0.5 * fx, m["y"] + 0.5 * fy, m["z"] + 0.5 * fz
    ux, uy, uz = jx * inv, jy * inv, jz * inv
    qx, qy, qz = jx * ux, jy * uy, jz * uz
    wx, wy, wz = ux * fx, uy * fy, uz * fz
    rho3 = rho * third
    base = third * (rho3 + (qx + qy + qz))
    wsum = wx + wy + wz
    wbase = (2.0 * third) * wsum
    equil = {
        "1": rho, "x": jx, "y": jy, "z": jz,
        "xy": jx * uy, "xz": jx * uz, "yz": jy * uz,
        "xx": rho3 + qx, "yy": rho3 + qy, "zz": rho3 + qz,
        "xyy": jx, "yxx": jy, "zxx": jz,
        "xxyy": base - 0.5 * qz, "xxzz": base - 0.5 * qy, "yyzz": base - 0.5 * qx,
    }
    source = {
        "1": None, "x": fx, "y": fy, "z": fz,
        "xy": fx * uy + fy * ux, "xz": fx * uz + fz * ux, "yz": fy * uz + fz * uy,
        "xx": wx, "yy": wy, "zz": wz,
        "xyy": fx, "yxx": fy, "zxx": fz,
        "xxyy": wbase - wz, "xxzz": wbase - wy, "yyzz": wbase - wx,
    }
    for table in (equil, source):
        table["xzz"], table["yzz"], table["zyy"] = table["xyy"], table["yxx"], table["zxx"]
    after = {}
    for row, name in enumerate(NAMES):
        after[name] = coef[0, row] * m[name] + coef[1, row] * equil[name]
        if source[name] is not None:
            after[name] = after[name] + coef[2, row] * source[name]
    return from_moments(after), (ux, uy, uz)


def kernel(
    counts, pop_hbm, mask_hbm, wet_hbm, wall_hbm, rate_hbm, out_hbm, vel_hbm,
    out_ref, vel_ref, pop_ref, mask_ref, wet_ref, wall_ref, rate_ref, coef,
    pot, f_buf, dens, bits, post, pot_ysend, pot_yrecv, pot_crecv,
    xa_recv, ya_send, ya_recv, xb_send, xb_recv, yb_send, yb_recv, cb_send, cb_recv,
    ox, oy, gx_d, gy_d, y_tile,
    in_sem, out_sem, pot_send_sem, pot_recv_sem, send_sem, recv_sem,
):
    nx, ny, nz = mask_ref.shape
    halves = ny // 8
    top = PAD + ny
    gx, gy = lax.axis_index("gx"), lax.axis_index("gy")
    SIGN = (-1, 1)
    leave_x, leave_y = (0, nx - 1), (0, ny - 1)
    enter_x, enter_y = (nx - 1, 0), (ny - 1, 0)
    ghost_x, ghost_y = (nx + 1, 0), (top, PAD - 1)
    XK = [ORDER[5:10], ORDER[0:5]]

    fetches = [
        pltpu.make_async_copy(a, b, in_sem.at[i])
        for i, (a, b) in enumerate(
            [
                (pop_hbm, pop_ref),
                (mask_hbm, mask_ref),
                (wet_hbm, wet_ref),
                (wall_hbm, wall_ref),
                (rate_hbm, rate_ref),
            ]
        )
    ]
    for copy in fetches:
        copy.start()

    def neighbour(d):
        return {
            "gx": lax.rem(gx + d[0] + counts[0], counts[0]),
            "gy": lax.rem(gy + d[1] + counts[1], counts[1]),
        }

    barrier = pltpu.get_barrier_semaphore()
    for d in SENDS:
        pl.semaphore_signal(
            barrier, inc=1, device_id=neighbour(d), device_id_type=pl.DeviceIdType.MESH
        )

    def remote(src, dst, sent, received, d):
        return pltpu.make_async_remote_copy(
            src_ref=src,
            dst_ref=dst,
            send_sem=sent,
            recv_sem=received,
            device_id=neighbour(d),
            device_id_type=pl.DeviceIdType.MESH,
        )

    rows = pl.ds(PAD, ny)
    xrows = pl.ds(PAD, nx)

    def pot_copies():
        pairs = {
            (1, 0): (pot.at[:, nx, rows], pot.at[:, 0, rows]),
            (-1, 0): (pot.at[:, 1, rows], pot.at[:, nx + 1, rows]),
        }
        for side, s in enumerate(SIGN):
            pairs[(0, s)] = (pot_ysend.at[side], pot_yrecv.at[side])
            for c, d in enumerate(CORNERS):
                if d[1] == s:
                    pairs[d] = (pot_ysend.at[side], pot_crecv.at[c])
        return [
            remote(*pairs[d], pot_send_sem.at[i], pot_recv_sem.at[i], d)
            for i, d in enumerate(SENDS)
        ]

    def a_copies(step, dim):
        p = step % 2
        made = []
        for m, s in enumerate(SIGN):
            if dim == "x":
                part = pl.ds(5 * (1 - m), 5)
                src = post.at[p, part, leave_x[m] + 1, rows]
                dst, i, d = xa_recv.at[step, m, :, rows], m, (s, 0)
            else:
                src = ya_send.at[step, m, :, xrows]
                dst, i, d = ya_recv.at[step, m, :, xrows], 2 + m, (0, s)
            made.append(remote(src, dst, send_sem.at[step, i], recv_sem.at[step, i], d))
        return made

    def b_copies(step, dim):
        made = []
        if dim == "corner":
            for c, d in enumerate(CORNERS):
                src, dst, i = cb_send.at[step, c], cb_recv.at[step, c], 8 + c
                made.append(remote(src, dst, send_sem.at[step, i], recv_sem.at[step, i], d))
        elif step < STEPS - 1:
            for m, s in enumerate(SIGN):
                if dim == "x":
                    src, dst, i, d = xb_send.at[step, m], xb_recv.at[step, m], 4 + m, (s, 0)
                else:
                    src, dst, i, d = yb_send.at[step, m], yb_recv.at[step, m], 6 + m, (0, s)
                made.append(remote(src, dst, send_sem.at[step, i], recv_sem.at[step, i], d))
        return made

    def clear():
        tile = jnp.zeros((8, nz), jnp.float32)
        for p in range(2):
            for m in range(2):
                for k in XK[m]:
                    for r in range((ny + 2 * PAD) // 8):
                        post[p, PLACE[k], ghost_x[m], pl.ds(8 * r, 8), :] = tile
                for k in CROSS[m]:
                    for x in range(nx):
                        post[p, PLACE[k], x + 1, pl.ds((top, 0)[m], 8), :] = tile
        for step in range(STEPS):
            for m in range(2):
                for j in range(5):
                    for r in (0, top):
                        xa_recv[step, m, j, pl.ds(r, 8), :] = tile
                    ya_send[step, m, j] = jnp.zeros((nx + 2 * PAD, nz), jnp.float32)
                    for r in (0, PAD + nx):
                        ya_recv[step, m, j, pl.ds(r, 8), :] = tile
                xb_send[step, m, pl.ds(ny, 8), :] = tile
                yb_send[step, m, 1] = jnp.zeros((nx, nz), jnp.float32)
            for c in range(4):
                cb_send[step, c] = tile

    def pot_unpack():
        for part in range(2):
            for m in range(2):
                for x in range(nx):
                    pot[part, x + 1, pl.ds(ghost_y[m], 1), :] = pot_yrecv[m, part, pl.ds(x, 1), :]
            for c, (sx, sy) in enumerate(CORNERS):
                mx, my = (sx + 1) // 2, (sy + 1) // 2
                pot[part, ghost_x[mx], pl.ds(ghost_y[my], 1), :] = pot_crecv[
                    c, part, pl.ds(leave_x[mx], 1), :
                ]

    def each_block(body, start=0, count=nx, stride=1):
        def plane(i, carry):
            for h in range(halves):
                body(start + i * stride, h)
            return carry

        lax.fori_loop(0, count, plane, 0)

    def first(x, h):
        block = pl.ds(8 * h, 8)
        fluid = mask_ref[x, block, :] == 1
        density = pop_ref[0, x, block, :]
        for k in range(1, 19):
            density = density + pop_ref[k, x, block, :]
        wet = wet_ref[x, block, :]
        wall = jnp.zeros_like(density)
        for c in range(WET_CLASSES):
            wall = wall + jnp.where(wet == c, wall_ref[c], 0.0)
        safe = jnp.where(fluid, density, 1.0)
        flag = jnp.where(fluid, 1.0, 0.0)
        for part, value in enumerate((jnp.where(fluid, 1.0 - jnp.exp(-safe), wall), flag)):
            pot[part, x + 1, pl.ds(PAD + 8 * h, 8), :] = value
            for m in range(2):
                if h == leave_y[m] // 8:
                    row = leave_y[m] % 8
                    pot_ysend[m, part, pl.ds(x, 1), :] = value[row : row + 1]

    def inflow(x, h):
        flags = jnp.zeros((8, nz), jnp.int32)
        for k, (ex, ey, ez) in enumerate(VEL):
            if k > 0:
                flag = roll_z(pot[1, x + 1 - ex, pl.ds(PAD + 8 * h - ey, 8), :], ez)
                flags = flags | jnp.where(flag == 1.0, 1 << k, 0)
        bits[x, pl.ds(8 * h, 8), :] = flags

    def collision(step, x, h):
        block = pl.ds(8 * h, 8)
        source = pop_ref if step == 0 else f_buf
        fluid = mask_ref[x, block, :] == 1
        near = lambda dx, dy: pot[0, x + 1 + dx, pl.ds(PAD + 8 * h + dy, 8), :]
        f, speed = collide([source[k, x, block, :] for k in range(19)], fluid, near, coef)
        for k in range(19):
            value = jnp.where(fluid, f[k], 0.0)
            post[step % 2, PLACE[k], x + 1, pl.ds(PAD + 8 * h, 8), :] = value
            for m in range(2):
                if k in CROSS[m] and h == leave_y[m] // 8:
                    row = leave_y[m] % 8
                    ya_send[step, m, CROSS[m].index(k), pl.ds(PAD + x, 1), :] = value[row : row + 1]
        if step == STEPS - 1:
            for c in range(3):
                vel_ref[c, x, block, :] = jnp.where(fluid, speed[c], 0.0)

    def stream(step, x, h):
        block, p = pl.ds(8 * h, 8), step % 2
        flags = bits[x, block, :]
        fluid = mask_ref[x, block, :] == 1
        density = None
        for k, (ex, ey, ez) in enumerate(VEL):
            if k == 0:
                value = post[p, PLACE[0], x + 1, pl.ds(PAD + 8 * h, 8), :]
            else:
                passed = roll_z(post[p, PLACE[k], x + 1 - ex, pl.ds(PAD + 8 * h - ey, 8), :], ez)
                bounced = post[p, PLACE[OPP[k]], x + 1, pl.ds(PAD + 8 * h, 8), :]
                value = jnp.where((flags & (1 << k)) != 0, passed, bounced)
            if step == STEPS - 1:
                out_ref[k, x, block, :] = jnp.where(fluid, value, 0.0)
            else:
                f_buf[k, x, block, :] = value
                density = value if density is None else density + value
        if step < STEPS - 1:
            dens[x, block, :] = density

    def x_sums(step):
        for m in range(2):
            for h in range(halves):
                total = None
                for k in XK[m]:
                    _, ey, ez = VEL[k]
                    value = roll_z(
                        post[step % 2, PLACE[k], leave_x[m] + 1, pl.ds(PAD + 8 * h - ey, 8), :], ez
                    )
                    total = value if total is None else total + value
                ox[m, pl.ds(8 * h, 8), :] = total

    def y_sums(step):
        for m in range(2):
            total = None
            for j, k in enumerate(CROSS[m]):
                ex, _, ez = VEL[k]
                value = roll_z(ya_send[step, m, j, pl.ds(PAD - ex, nx), :], ez)
                total = value if total is None else total + value
            oy[m] = total

    one = lambda i: pl.ds(i, 1)

    def pack_x(step):
        for m in range(2):
            xb_send[step, m, pl.ds(0, ny), :] = dens[leave_x[m]]
            for n in range(2):
                xb_send[step, m, one(ny + n), :] = oy[n, one(leave_x[m]), :]
        for c, (sx, sy) in enumerate(CORNERS):
            mx, my = (sx + 1) // 2, (sy + 1) // 2
            cb_send[step, c, 1:2, :] = dens[leave_x[mx], one(leave_y[my]), :]
            cb_send[step, c, 2:3, :] = oy[my, one(leave_x[mx]), :]
            cb_send[step, c, 3:4, :] = ox[mx, one(leave_y[my]), :]

    def pack_y(step):
        for m in range(2):
            for n in range(2):
                yb_send[step, m, 1, one(n), :] = ox[n, one(leave_y[m]), :]
            for x in range(nx):
                yb_send[step, m, 0, one(x), :] = dens[x, one(leave_y[m]), :]

    def pack_corners(step):
        for c, (sx, sy) in enumerate(CORNERS):
            mx, my = (sx + 1) // 2, (sy + 1) // 2
            j = CROSS[my].index(INDEX[(sx, sy, 0)])
            cb_send[step, c, 0:1, :] = ya_send[step, my, j, pl.ds(PAD + leave_x[mx], 1), :]

    def arrive(step, k, x, block, value):
        if step == STEPS - 1:
            fluid = mask_ref[x, block, :] == 1
            out_ref[k, x, block, :] = out_ref[k, x, block, :] + jnp.where(fluid, value, 0.0)
        else:
            f_buf[k, x, block, :] = f_buf[k, x, block, :] + value

    def x_arrive(step):
        for m in range(2):
            x = enter_x[m]
            for h in range(halves):
                block = pl.ds(8 * h, 8)
                total = None
                for j, k in enumerate(XK[m]):
                    _, ey, ez = VEL[k]
                    value = roll_z(xa_recv[step, m, j, pl.ds(PAD + 8 * h - ey, 8), :], ez)
                    arrive(step, k, x, block, value)
                    total = value if total is None else total + value
                if step < STEPS - 1:
                    dens[x, block, :] = dens[x, block, :] + total

    def y_arrive(step):
        for m in range(2):
            row = pl.ds(enter_y[m], 1)
            total = None
            for j, k in enumerate(CROSS[m]):
                ex, _, ez = VEL[k]
                value = roll_z(ya_recv[step, m, j, pl.ds(PAD - ex, nx), :], ez)
                y_tile[m, j] = value
                total = value if total is None else total + value
            y_tile[m, 5] = total
            for x in range(nx):
                for j, k in enumerate(CROSS[m]):
                    arrive(step, k, x, row, y_tile[m, j, pl.ds(x, 1), :])
                if step < STEPS - 1:
                    dens[x, row, :] = dens[x, row, :] + y_tile[m, 5, pl.ds(x, 1), :]

    def own_potential(x, h):
        block, where = pl.ds(8 * h, 8), pl.ds(PAD + 8 * h, 8)
        fluid = mask_ref[x, block, :] == 1
        value = 1.0 - jnp.exp(-dens[x, block, :])
        pot[0, x + 1, where, :] = jnp.where(fluid, value, pot[0, x + 1, where, :])

    def corners_arrive(step):
        for c, (sx, sy) in enumerate(CORNERS):
            mx, my = (sx + 1) // 2, (sy + 1) // 2
            x, y = enter_x[mx], enter_y[my]
            row = pl.ds(y, 1)
            value = cb_recv[step, c, 0:1, :]
            arrive(step, INDEX[(sx, sy, 0)], x, row, value)
            if step < STEPS - 1:
                dens[x, row, :] = dens[x, row, :] + value

    def ghost_potential(step):
        def put(x, where, density):
            flag = pot[1, x, where, :] == 1.0
            pot[0, x, where, :] = jnp.where(flag, 1.0 - jnp.exp(-density), pot[0, x, where, :])

        for m in range(2):
            gx_d[m] = xb_recv[step, m, pl.ds(0, ny), :] + ox[1 - m]
            gy_d[m] = yb_recv[step, m, 0] + oy[1 - m]
        for c, (sx, sy) in enumerate(CORNERS):
            mx, my = (sx + 1) // 2, (sy + 1) // 2
            x, y = enter_x[mx], enter_y[my]
            j = CROSS[my].index(INDEX[(-sx, sy, 0)])
            gx_d[mx, one(y), :] = gx_d[mx, one(y), :] + (
                ya_recv[step, my, j, one(PAD + x), :] + cb_recv[step, c, 2:3, :]
            )
            j = XK[mx].index(INDEX[(sx, -sy, 0)])
            gy_d[my, one(x), :] = gy_d[my, one(x), :] + (
                xa_recv[step, mx, j, one(PAD + y), :] + cb_recv[step, c, 3:4, :]
            )
            j = CROSS[1 - my].index(INDEX[(-sx, -sy, 0)])
            density = (
                cb_recv[step, c, 1:2, :] + ya_send[step, 1 - my, j, one(PAD + x), :]
            ) + (xb_recv[step, mx, one(ny + 1 - my), :] + yb_recv[step, my, 1, one(1 - mx), :])
            put(ghost_x[mx], one(ghost_y[my]), density)
        for m in range(2):
            for h in range(halves):
                put(ghost_x[m], pl.ds(PAD + 8 * h, 8), gx_d[m, pl.ds(8 * h, 8), :])
            gy_d[m] = 1.0 - jnp.exp(-gy_d[m])
            for x in range(nx):
                where = one(ghost_y[m])
                flag = pot[1, x + 1, where, :] == 1.0
                pot[0, x + 1, where, :] = jnp.where(
                    flag, gy_d[m, one(x), :], pot[0, x + 1, where, :]
                )

    for copy in fetches:
        copy.wait()
    for row in range(19):
        rate = rate_ref[row]
        coef[0, row] = 1.0 - rate
        coef[1, row] = rate * EQUIL_SCALE[row]
        coef[2, row] = (1.0 - 0.5 * rate) * SOURCE_SCALE[row]
    each_block(first)
    pl.semaphore_wait(barrier, len(SENDS))

    def start(group, swapped=()):
        if swapped:
            @pl.when(gx == counts[0] - 1)
            def _():
                for copy in swapped:
                    copy.start()

            @pl.when(gx != counts[0] - 1)
            def _():
                for copy in group:
                    copy.start()
        else:
            for copy in group:
                copy.start()
        return group

    def finish(group):
        for copy in group:
            copy.wait()

    def start_pot():
        group = pot_copies()
        order = [1, 0, 6, 7, 4, 5, 2, 3]
        return start([group[i] for i in order], [group[i] for i in (0, 1, 4, 5, 6, 7, 2, 3)])

    def start_a(step):
        group = a_copies(step, "x")
        return start(group, group[::-1])

    def start_b(step):
        group, corners = b_copies(step, "x"), b_copies(step, "corner")
        return start(group + corners[::-1], group[::-1] + corners)

    moving = start_pot()
    clear()
    finish(moving)
    pot_unpack()
    EDGE, NEXT, INNER = (0, 2, nx - 1), (1, 2, nx - 3), (2, nx - 4, 1)
    WITHIN = (1, nx - 2, 1)
    for step in range(STEPS):
        final = step == STEPS - 1
        hit = functools.partial(collision, step)
        move = functools.partial(stream, step)
        each_block(hit, *EDGE)
        x_moving = start_a(step)
        pack_corners(step)
        if not final:
            each_block(hit, *NEXT)
            if step == 0:
                each_block(inflow, *EDGE)
            each_block(move, *EDGE)
            x_sums(step)
            y_sums(step)
            pack_x(step)
        b_moving = start_b(step)
        if step == 0:
            each_block(inflow, *WITHIN)
        if final:
            each_block(hit, *NEXT)
        each_block(hit, *INNER)
        y_moving = start(a_copies(step, "y"))
        if final:
            leaving = [pltpu.make_async_copy(vel_ref, vel_hbm, out_sem.at[0])]
            leaving[0].start()
            each_block(move)
        else:
            each_block(move, *WITHIN)
            y_sums(step)
            pack_y(step)
            b_moving += start(b_copies(step, "y"))
        finish(y_moving)
        y_arrive(step)
        if final:
            for i, (x, count) in enumerate([(1, nx - 2), (0, 1), (nx - 1, 1)]):
                where = pl.ds(x, count)
                leaving.append(
                    pltpu.make_async_copy(
                        out_ref.at[:, where], out_hbm.at[:, where], out_sem.at[1 + i]
                    )
                )
            leaving[1].start()
        else:
            each_block(own_potential, *WITHIN)
        finish(x_moving)
        x_arrive(step)
        finish(b_moving)
        corners_arrive(step)
        if final:
            leaving[2].start()
            leaving[3].start()
            finish(leaving)
        else:
            each_block(own_potential, *EDGE)
            ghost_potential(step)


CHUNK = 5


def hand_over(pop_in, vel_in, pop_out, vel_out, pop, vel, in_sem, out_sem):
    parts = [(pop_in, pop, pop_out, k) for k in range(0, pop_in.shape[0], CHUNK)]
    parts.append((vel_in, vel, vel_out, 0))
    inward, outward = [], []
    for i, (src, held, dst, k) in enumerate(parts):
        where = pl.ds(k, min(CHUNK, src.shape[0] - k))
        inward.append(pltpu.make_async_copy(src.at[where], held.at[where], in_sem.at[i]))
        outward.append(pltpu.make_async_copy(held.at[where], dst.at[where], out_sem.at[i]))
    for copy in inward:
        copy.start()
    for arriving, leaving in zip(inward, outward):
        arriving.wait()
        leaving.start()
    for copy in outward:
        copy.wait()


def per_device(counts, populations, fluid_mask, wet_class, wall_potential, relax_rates):
    nx, ny, nz = fluid_mask.shape
    hbm = pl.BlockSpec(memory_space=pltpu.HBM)
    f32 = jnp.float32
    padded = (nx + 2, ny + 2 * PAD, nz)
    shapes = (
        jax.ShapeDtypeStruct((19, nx, ny, nz), f32),
        jax.ShapeDtypeStruct((3, nx, ny, nz), f32),
    )
    results = pl.pallas_call(
        functools.partial(kernel, counts),
        out_shape=shapes,
        in_specs=[hbm] * 5,
        out_specs=(hbm, hbm),
        scratch_shapes=[
            pltpu.VMEM((19, nx, ny, nz), f32),
            pltpu.VMEM((3, nx, ny, nz), f32),
            pltpu.VMEM(populations.shape, f32),
            pltpu.VMEM(fluid_mask.shape, jnp.int32),
            pltpu.VMEM(wet_class.shape, jnp.int32),
            pltpu.SMEM(wall_potential.shape, f32),
            pltpu.SMEM(relax_rates.shape, f32),
            pltpu.SMEM((3,) + relax_rates.shape, f32),
            pltpu.VMEM((2,) + padded, f32),
            pltpu.VMEM((19, nx, ny, nz), f32),
            pltpu.VMEM((nx, ny, nz), f32),
            pltpu.VMEM((nx, ny, nz), jnp.int32),
            pltpu.VMEM((2, 19) + padded, f32),
            pltpu.VMEM((2, 2, nx, nz), f32),
            pltpu.VMEM((2, 2, nx, nz), f32),
            pltpu.VMEM((4, 2, nx, nz), f32),
            pltpu.VMEM((STEPS, 2, 5, ny + 2 * PAD, nz), f32),
            pltpu.VMEM((STEPS, 2, 5, nx + 2 * PAD, nz), f32),
            pltpu.VMEM((STEPS, 2, 5, nx + 2 * PAD, nz), f32),
            pltpu.VMEM((STEPS, 2, ny + 8, nz), f32),
            pltpu.VMEM((STEPS, 2, ny + 8, nz), f32),
            pltpu.VMEM((STEPS, 2, 2, nx, nz), f32),
            pltpu.VMEM((STEPS, 2, 2, nx, nz), f32),
            pltpu.VMEM((STEPS, 4, 8, nz), f32),
            pltpu.VMEM((STEPS, 4, 8, nz), f32),
            pltpu.VMEM((2, ny, nz), f32),
            pltpu.VMEM((2, nx, nz), f32),
            pltpu.VMEM((2, ny, nz), f32),
            pltpu.VMEM((2, nx, nz), f32),
            pltpu.VMEM((2, 6, nx, nz), f32),
            pltpu.SemaphoreType.DMA((5,)),
            pltpu.SemaphoreType.DMA((4,)),
            pltpu.SemaphoreType.DMA((8,)),
            pltpu.SemaphoreType.DMA((8,)),
            pltpu.SemaphoreType.DMA((STEPS, 12)),
            pltpu.SemaphoreType.DMA((STEPS, 12)),
        ],
        compiler_params=pltpu.CompilerParams(
            collective_id=0, has_side_effects=True, vmem_limit_bytes=60 * 1024 * 1024
        ),
    )(populations, fluid_mask, wet_class, wall_potential, relax_rates)
    return pl.pallas_call(
        hand_over,
        out_shape=shapes,
        in_specs=[hbm] * 2,
        out_specs=(hbm, hbm),
        scratch_shapes=[pltpu.VMEM(shape.shape, f32) for shape in shapes]
        + [pltpu.SemaphoreType.DMA((-(-19 // CHUNK) + 1,))] * 2,
        compiler_params=pltpu.CompilerParams(vmem_limit_bytes=60 * 1024 * 1024),
    )(*results)


def solution(mesh):
    counts = (mesh.shape["gx"], mesh.shape["gy"])
    return jax.shard_map(
        functools.partial(per_device, counts),
        mesh=mesh,
        in_specs=(
            P(None, ("groups", "gx"), "gy", None),
            P(("groups", "gx"), "gy", None),
            P(("groups", "gx"), "gy", None),
            P("groups"),
            P(),
        ),
        out_specs=(P(None, ("groups", "gx"), "gy", None), P(None, ("groups", "gx"), "gy", None)),
        check_vma=False,
    )
```

profile of v0, /device:TPU:1, one launch (start us, length us, event | category | flops | bytes accessed | tf_op | source)
XLA Modules:
  0.0 37.1 jit_solution(9992402840819199832)
XLA Ops:
  0.6 34.3 %shard_map.68 = (f32[19,8,16,128]{3,2,1,0:T(8,128)}, f32[3,8,16,128]{3,2,1,0:T(8,128)}) custom-call(f32[19,8,16,128]{3,2,1,0:T(8,128)} %pop_hbm.1, s32[8,16,128]{2,1,0:T(8,128)} %mask_hbm.1, s32[8,16,128]{2,1,0:T(8,128)} %wet_hbm.1, f32[4]{0:T(128)} %wall_hbm.1, f32[19]{0:T(128)} %rate_hbm.1), custom_call_target="tpu_custom_call" | custom-call | tf_op jit(solution)/shard_map/pallas_call | solution.py:645
  35.0 2.1 %shard_map.69 = (f32[19,8,16,128]{3,2,1,0:T(8,128)}, f32[3,8,16,128]{3,2,1,0:T(8,128)}) custom-call(f32[19,8,16,128]{3,2,1,0:T(8,128)} %get-tuple-element.4.pop_in, f32[3,8,16,128]{3,2,1,0:T(8,128)} %get-tuple-element.5.vel_in), custom_call_target="tpu_custom_call" | custom-call | tf_op jit(solution)/shard_map/pallas_call | solution.py:692
where the time goes:
time: 37.3 us; the launch traced here: 37.1 us
  Pallas kernels  36.5 us (98%)
  between operations  0.64 us (2%)
    pallas_call x1, Pallas kernels, per_device(): pl.pallas_call(functools.partial(kernel, counts), out_shape=shapes, in_sp...  34.3 us
    pallas_call x1, Pallas kernels, per_device(): pl.pallas_call(hand_over, out_shape=shapes, in_specs=[hbm] * 2, out_specs...  2.15 us

commit v1 on v0

--- a/solution.py
+++ b/solution.py
@@ -300,13 +300,19 @@
                     c, part, pl.ds(leave_x[mx], 1), :
                 ]
 
-    def each_block(body, start=0, count=nx, stride=1):
-        def plane(i, carry):
-            for h in range(halves):
-                body(start + i * stride, h)
+    def each_block(body, start=0, count=nx, stride=1, group=1):
+        group = group if count % group == 0 else 1
+
+        def planes(i, carry):
+            for j in range(group):
+                for h in range(halves):
+                    body(start + (i * group + j) * stride, h)
             return carry
 
-        lax.fori_loop(0, count, plane, 0)
+        if count == group:
+            planes(0, 0)
+        else:
+            lax.fori_loop(0, count // group, planes, 0)
 
     def first(x, h):
         block = pl.ds(8 * h, 8)
@@ -560,11 +566,11 @@
         final = step == STEPS - 1
         hit = functools.partial(collision, step)
         move = functools.partial(stream, step)
-        each_block(hit, *EDGE)
+        each_block(hit, *EDGE, group=2)
         x_moving = start_a(step)
         pack_corners(step)
         if not final:
-            each_block(hit, *NEXT)
+            each_block(hit, *NEXT, group=2)
             if step == 0:
                 each_block(inflow, *EDGE)
             each_block(move, *EDGE)
@@ -575,8 +581,8 @@
         if step == 0:
             each_block(inflow, *WITHIN)
         if final:
-            each_block(hit, *NEXT)
-        each_block(hit, *INNER)
+            each_block(hit, *NEXT, group=2)
+        each_block(hit, *INNER, group=2)
         y_moving = start(a_copies(step, "y"))
         if final:
             leaving = [pltpu.make_async_copy(vel_ref, vel_hbm, out_sem.at[0])]

time: 37.3 us -> 36.8 us (0.987)
  Pallas kernels: 36.5 us -> 36 us
    pallas_call x1, Pallas kernels: 34.3 us -> 33.8 us  [per_device(): pl.pallas_call(functools.partial(kernel, counts), out_shape=shapes, in_sp...]
where the time goes in v1:
time: 36.8 us; the launch traced here: 36.6 us
  Pallas kernels  36 us (98%)
  between operations  0.64 us (2%)
    pallas_call x1, Pallas kernels, per_device(): pl.pallas_call(functools.partial(kernel, counts), out_shape=shapes, in_sp...  33.8 us
    pallas_call x1, Pallas kernels, per_device(): pl.pallas_call(hand_over, out_shape=shapes, in_specs=[hbm] * 2, out_specs...  2.15 us

profile of v1, /device:TPU:1, one launch (start us, length us, event | category | flops | bytes accessed | tf_op | source)
XLA Modules:
  0.0 36.6 jit_solution(2512476744909316996)
XLA Ops:
  0.6 33.8 %shard_map.68 = (f32[19,8,16,128]{3,2,1,0:T(8,128)}, f32[3,8,16,128]{3,2,1,0:T(8,128)}) custom-call(f32[19,8,16,128]{3,2,1,0:T(8,128)} %pop_hbm.1, s32[8,16,128]{2,1,0:T(8,128)} %mask_hbm.1, s32[8,16,128]{2,1,0:T(8,128)} %wet_hbm.1, f32[4]{0:T(128)} %wall_hbm.1, f32[19]{0:T(128)} %rate_hbm.1), custom_call_target="tpu_custom_call" | custom-call | tf_op jit(solution)/shard_map/pallas_call | solution.py:651
  34.5 2.1 %shard_map.69 = (f32[19,8,16,128]{3,2,1,0:T(8,128)}, f32[3,8,16,128]{3,2,1,0:T(8,128)}) custom-call(f32[19,8,16,128]{3,2,1,0:T(8,128)} %get-tuple-element.4.pop_in, f32[3,8,16,128]{3,2,1,0:T(8,128)} %get-tuple-element.5.vel_in), custom_call_target="tpu_custom_call" | custom-call | tf_op jit(solution)/shard_map/pallas_call | solution.py:698
